TPU v7x, 512 devices: a whole 4x8x8 slice. The times are simulated.
512 devices in a mesh: sub: 64 (over y, z_lo, core), grp: 8 (over x, z_hi).
Axes of the slice: x: 4, y: 8, z: 8 (z_hi: 2, z_lo: 4; z = z_hi * 4 + z_lo), core: 2. Of those that a mesh axis runs over, the one named last changes fastest.
Arguments:
- front_trail: float32 [16384, 16384], P('sub', 'grp'), may hold values from -6 to 6
- front_below: float32 [16384, 1024], P('sub', 'grp'), may hold values from -6 to 6
- front_pivot: float32 [1024, 1024], P('sub', 'grp'), may hold values from -0.02 to 5, as said below
- panel_mask: int32 [64], P('sub'), may hold values 0 or 1
- child_tiles: float32 [64, 8, 2, 256, 256], P('sub', 'grp'), may hold values from -6 to 6
- child_slot: int32 [64, 8, 2], P('sub', 'grp'), may hold values from 0 to 7
- child_far: int32 [64, 8, 2], P('sub', 'grp'), may hold values 0 or 1
Outputs:
- schur_block: float32 [16384, 16384], P('sub', 'grp')
- panel: float32 [16384, 1024], P('sub', 'grp')
Inputs may be any that keep to these rules, and one draw needn't show every extreme that they name: `front_pivot`: symmetric positive definite.
All inputs are finite; a program needn't handle non-finite values. No bound on the sum of `panel_mask` or of `child_far` on one device may be relied on, other than what follows from the above.
Results may differ from a plain program's by a relative error of at most 0.0018.
The roundings to bfloat16 on the way count: a program that leaves them out, or rounds other values in their place, can miss the bound.
Values may be sent and summed in bfloat16 or wider, within the bound.
A program may use at most 128 MiB of HBM per device.

v0:
```python
import jax
import jax.numpy as jnp
from jax import lax
from jax.sharding import PartitionSpec as P


def from_partner(value, axis, distance):
    return lax.ppermute(value, axis, [(i, i ^ 1 << distance) for i in range(lax.axis_size(axis))])


def spread_tiles(tile_data, slot_ids, weights, slot_count, tiles_row, tiles_col, tile_size):
    onehot = (slot_ids[:, None] == jnp.arange(slot_count, dtype=jnp.int32)[None, :]).astype(
        jnp.float32
    )
    onehot = onehot * weights[:, None]
    tile_grid = jnp.einsum("uk,uab->kab", onehot, tile_data, precision=lax.Precision.HIGHEST)
    tile_grid = tile_grid.reshape(tiles_row, tiles_col, tile_size, tile_size).transpose(0, 2, 1, 3)
    return tile_grid.reshape(tiles_row * tile_size, tiles_col * tile_size)


def body(front_trail, front_below, front_pivot, panel_mask, child_tiles, child_slot, child_far):
    rows_dev, cols_dev = front_trail.shape
    tile_size = child_tiles.shape[-1]
    tiles_row = rows_dev // tile_size
    tiles_col = cols_dev // tile_size
    slot_count = tiles_row * tiles_col
    n_sub = lax.axis_size("sub")
    top_bit = n_sub.bit_length() - 2
    tile_data = child_tiles.reshape(-1, tile_size, tile_size)
    slot_ids = child_slot.reshape(-1)
    far_flag = child_far.reshape(-1).astype(jnp.float32)
    near_part = spread_tiles(
        tile_data, slot_ids, 1.0 - far_flag, slot_count, tiles_row, tiles_col, tile_size
    )
    outgoing = spread_tiles(
        tile_data, slot_ids, far_flag, slot_count, tiles_row, tiles_col, tile_size
    )
    far_part = from_partner(outgoing.astype(jnp.bfloat16), "sub", top_bit).astype(outgoing.dtype)
    partial_value = lax.all_gather(front_pivot, "sub", axis=0, tiled=True)
    whole_pivot = lax.all_gather(partial_value, "grp", axis=1, tiled=True)
    width = whole_pivot.shape[0]
    factor = jnp.linalg.cholesky(whole_pivot)
    inverse = jax.scipy.linalg.solve_triangular(
        factor, jnp.eye(width, dtype=jnp.float32), lower=True
    )
    row_keep = jnp.repeat(panel_mask, tile_size).astype(jnp.float32)
    masked = front_below * row_keep[:, None]
    full_rows = lax.all_gather(masked, "grp", axis=1, tiled=True)
    piece_cols = front_below.shape[1]
    inverse_rows = lax.dynamic_slice_in_dim(
        inverse, lax.axis_index("grp") * piece_cols, piece_cols, 0
    )
    panel_piece = lax.dot_general(
        full_rows,
        inverse_rows,
        (((1,), (1,)), ((), ())),
        precision=lax.Precision.HIGHEST,
        preferred_element_type=jnp.float32,
    )
    rounded_piece = panel_piece.astype(jnp.bfloat16)
    own_rows = lax.all_gather(rounded_piece, "grp", axis=1, tiled=True)
    every_row = lax.all_gather(rounded_piece, "sub", axis=0, tiled=True)
    mine_rows = lax.all_to_all(every_row, "grp", split_axis=0, concat_axis=1, tiled=True)
    update = lax.dot_general(
        own_rows, mine_rows, (((1,), (1,)), ((), ())), preferred_element_type=jnp.float32
    )
    schur_block = front_trail + near_part + far_part - update
    return (schur_block, panel_piece)


def solution(mesh):
    return jax.shard_map(
        body,
        mesh=mesh,
        in_specs=(
            P("sub", "grp"),
            P("sub", "grp"),
            P("sub", "grp"),
            P("sub"),
            P("sub", "grp", None, None, None),
            P("sub", "grp", None),
            P("sub", "grp", None),
        ),
        out_specs=(P("sub", "grp"), P("sub", "grp")),
        check_vma=False,
    )
```

profile of v0, /device:TPU:64, one launch (start us, length us, event | category | flops | bytes accessed | tf_op | source)
XLA Modules:
  0.0 838.1 jit_solution(6582451614089924089)
XLA Ops:
  7.2 80.4 %all_gather.16 = f32[1024,128]{1,0:T(8,128)S(1)} all-gather(f32[16,128]{1,0:T(8,128)} %param.9), channel_id=1, replica_groups=mesh['sub'=64,'grp'=8] {'sub'}, dimensions={0}, use_global_device_ids=true | all-gather | bytes 532480 | tf_op jit(solution)/shard_map/all_gather | solution.py:39
  89.3 1.6 broadcast_multiply_fusion
  91.3 2.4 fusion.21
  93.8 107.5 %all-gather.6.cloned.1.call-done = f32[1024,1024]{0,1:T(8,128)} async-done(((f32[1024,128]{0,1:T(8,128)}), f32[1024,1024]{0,1:T(8,128)}) %all-gather.6.cloned.1.call-update) | async-done | bytes 4194320 | tf_op jit(solution)/shard_map/all_gather | solution.py:40
  201.3 5.3 copy.21
  206.6 4.4 fusion
  211.0 2.0 copy-done.2
  213.0 11.7 %cholesky.223 = f32[128,128]{1,0:T(8,128)S(1)} custom-call(f32[128,128]{1,0:T(8,128)S(1)} %cholesky.580), custom_call_target="Cholesky" | custom-call | tf_op jit(solution)/shard_map/jit(cholesky)/cholesky | solution.py:42
  224.8 9.8 %custom-call.63 = f32[1,128,128]{1,2,0:T(8,128)S(1)} custom-call(f32[1,128,128]{2,1,0:T(8,128)S(1)} %get-tuple-element.66), custom_call_target="InvertDiagBlocksLowerTriangular" | custom-call | tf_op jit(solution)/shard_map/jit(cholesky)/cholesky | solution.py:42
  234.6 2.5 cholesky.255
  237.1 2.3 constant_dynamic-update-slice_fusion.32
  239.4 1.5 convolution_subtract_fusion.5
  241.0 12.0 %cholesky.244 = f32[128,128]{1,0:T(8,128)S(1)} custom-call(f32[128,128]{1,0:T(8,128)S(1)} %cholesky.584), custom_call_target="Cholesky" | custom-call | tf_op jit(solution)/shard_map/jit(cholesky)/cholesky | solution.py:42
  253.7 9.8 %custom-call.64 = f32[1,128,128]{1,2,0:T(8,128)S(1)} custom-call(f32[1,128,128]{2,1,0:T(8,128)S(1)} %get-tuple-element.63), custom_call_target="InvertDiagBlocksLowerTriangular" | custom-call | tf_op jit(solution)/shard_map/jit(cholesky)/cholesky | solution.py:42
  264.7 2.1 convolution_subtract_fusion.6
  266.8 11.7 %cholesky.468 = f32[128,128]{1,0:T(8,128)S(1)} custom-call(f32[128,128]{1,0:T(8,128)S(1)} %cholesky.589), custom_call_target="Cholesky" | custom-call | tf_op jit(solution)/shard_map/jit(cholesky)/cholesky | solution.py:42
  279.8 9.8 %custom-call.65 = f32[1,128,128]{1,2,0:T(8,128)S(1)} custom-call(f32[1,128,128]{2,1,0:T(8,128)S(1)} %get-tuple-element.60), custom_call_target="InvertDiagBlocksLowerTriangular" | custom-call | tf_op jit(solution)/shard_map/jit(cholesky)/cholesky | solution.py:42
  290.8 2.3 convolution_subtract_fusion.7
  293.2 11.8 %cholesky.487 = f32[128,128]{1,0:T(8,128)S(1)} custom-call(f32[128,128]{1,0:T(8,128)S(1)} %cholesky.594), custom_call_target="Cholesky" | custom-call | tf_op jit(solution)/shard_map/jit(cholesky)/cholesky | solution.py:42
  306.3 9.8 %custom-call.66 = f32[1,128,128]{1,2,0:T(8,128)S(1)} custom-call(f32[1,128,128]{2,1,0:T(8,128)S(1)} %get-tuple-element.57), custom_call_target="InvertDiagBlocksLowerTriangular" | custom-call | tf_op jit(solution)/shard_map/jit(cholesky)/cholesky | solution.py:42
  317.2 2.4 convolution_subtract_fusion.8
  319.6 11.7 %cholesky.506 = f32[128,128]{1,0:T(8,128)S(1)} custom-call(f32[128,128]{1,0:T(8,128)S(1)} %cholesky.599), custom_call_target="Cholesky" | custom-call | tf_op jit(solution)/shard_map/jit(cholesky)/cholesky | solution.py:42
  332.6 10.0 %custom-call.67 = f32[1,128,128]{1,2,0:T(8,128)S(1)} custom-call(f32[1,128,128]{2,1,0:T(8,128)S(1)} %get-tuple-element.54), custom_call_target="InvertDiagBlocksLowerTriangular" | custom-call | tf_op jit(solution)/shard_map/jit(cholesky)/cholesky | solution.py:42
  343.6 2.3 convolution_subtract_fusion.9
  345.9 11.7 %cholesky.526 = f32[128,128]{1,0:T(8,128)S(1)} custom-call(f32[128,128]{1,0:T(8,128)S(1)} %cholesky.604), custom_call_target="Cholesky" | custom-call | tf_op jit(solution)/shard_map/jit(cholesky)/cholesky | solution.py:42
  358.9 9.8 %custom-call.68 = f32[1,128,128]{1,2,0:T(8,128)S(1)} custom-call(f32[1,128,128]{2,1,0:T(8,128)S(1)} %get-tuple-element.51), custom_call_target="InvertDiagBlocksLowerTriangular" | custom-call | tf_op jit(solution)/shard_map/jit(cholesky)/cholesky | solution.py:42
  369.6 2.0 convolution_subtract_fusion.10
  371.7 12.1 %cholesky.546 = f32[128,128]{1,0:T(8,128)S(1)} custom-call(f32[128,128]{1,0:T(8,128)S(1)} %cholesky.609), custom_call_target="Cholesky" | custom-call | tf_op jit(solution)/shard_map/jit(cholesky)/cholesky | solution.py:42
  385.1 9.8 %custom-call.69 = f32[1,128,128]{1,2,0:T(8,128)S(1)} custom-call(f32[1,128,128]{2,1,0:T(8,128)S(1)} %get-tuple-element.48), custom_call_target="InvertDiagBlocksLowerTriangular" | custom-call | tf_op jit(solution)/shard_map/jit(cholesky)/cholesky | solution.py:42
  395.8 1.8 convolution_subtract_fusion.11
  397.6 11.7 %cholesky.564 = f32[128,128]{1,0:T(8,128)S(1)} custom-call(f32[128,128]{1,0:T(8,128)S(1)} %convolution_subtract_fusion.11), custom_call_target="Cholesky" | custom-call | tf_op jit(solution)/shard_map/jit(cholesky)/cholesky | solution.py:42
  416.1 4.8 select_select_fusion
  421.0 22.6 %while.1 = (s32[]{:T(128)}, f32[1024,1024]{1,0:T(8,128)}, s32[8,2]{0,1:T(2,128)S(1)}, f32[8,128,128]{2,1,0:T(8,128)S(1)}, s32[]{:T(128)}) while((s32[]{:T(128)}, f32[1024,1024]{1,0:T(8,128)}, s32[8,2]{0,1:T(2,128)S(1)}, f32[8,128,128]{2,1,0:T(8,128)S(1)}, s32[]{:T(128)}) %tuple.62), condition=%wide.while_cond, body=%wide.while_body.sunk | while | flops 2 | bytes 131181 | solution.py:43
  421.6 2.2 bitcast_dynamic-update-slice_fusion.2
  424.4 2.2 bitcast_dynamic-update-slice_fusion.2
  427.2 2.2 bitcast_dynamic-update-slice_fusion.2
  430.1 2.2 bitcast_dynamic-update-slice_fusion.2
  432.9 2.2 bitcast_dynamic-update-slice_fusion.2
  435.7 2.2 bitcast_dynamic-update-slice_fusion.2
  438.5 2.2 bitcast_dynamic-update-slice_fusion.2
  441.4 2.1 bitcast_dynamic-update-slice_fusion.2
  443.5 78.8 %custom-call.70 = f32[8,128,128]{1,2,0:T(8,128)S(1)} custom-call(f32[8,128,128]{2,1,0:T(8,128)S(1)} %get-tuple-element.9), custom_call_target="InvertDiagBlocksLowerTriangular" | custom-call | tf_op jit(solution)/shard_map/jit(_solve_triangular)/triangular_solve | solution.py:43
  523.7 1.7 convolution_subtract_fusion.4
  525.4 1.6 constant_dynamic-update-slice_fusion.16
  527.0 1.6 convolution_subtract_fusion
  528.7 1.5 constant_dynamic-update-slice_fusion.15
  530.2 2.0 fusion.15
  532.2 1.5 constant_dynamic-update-slice_fusion.14
  533.8 2.2 fusion.18
  536.0 1.5 constant_dynamic-update-slice_fusion.13
  537.6 2.6 convolution_subtract_fusion.2
  540.2 1.5 constant_dynamic-update-slice_fusion.12
  541.7 2.8 convolution_subtract_fusion.1
  546.0 3.5 convolution_subtract_fusion.3
  549.4 1.4 convolution_dynamic-update-slice_fusion
  550.9 3.0 fusion.89
  553.9 117.1 %all-gather.8.cloned.1.call-done = bf16[16384,128]{1,0:T(8,128)(2,1)} async-done(((bf16[256,128]{1,0:T(8,128)(2,1)}), bf16[16384,128]{1,0:T(8,128)(2,1)}) %all-gather.8.cloned.1.call-update) | async-done | bytes 4194320 | tf_op jit(solution)/shard_map/all_gather | solution.py:62
  671.0 6.5 copy.22
  677.5 8.8 %all-to-all-start = ((bf16[8,2048,128]{1,2,0:T(8,128)(2,1)}), bf16[8,2048,128]{1,2,0:T(8,128)(2,1)}, u32[]{:S(2)}, u32[]{:S(2)}) async-start(bf16[8,2048,128]{1,2,0:T(8,128)(2,1)} %copy.22), calls=%async_computation | async-start | bytes 8388608 | tf_op jit(solution)/shard_map/all_to_all | solution.py:63
  686.4 2.5 convolution_convert_fusion
  689.2 5.3 collective-permute-start
  694.5 2.5 fusion.39
  698.0 127.4 %all_gather.18 = bf16[256,1024]{1,0:T(8,128)(2,1)S(1)} all-gather(bf16[256,128]{1,0:T(8,128)(2,1)S(1)} %copy-done.3), channel_id=1, replica_groups=mesh['sub'=64,'grp'=8] {'grp'}, dimensions={1}, use_global_device_ids=true | all-gather | bytes 589824 | tf_op jit(solution)/shard_map/all_gather | solution.py:61
  825.4 5.8 add_subtract_fusion
  (75 shorter events, 25.7 us)
Async XLA Ops:
  7.2 679.2 %copy-start = (f32[1,1,2,256,256]{4,3,2,1,0:T(8,128)S(1)}, f32[1,1,2,256,256]{4,3,2,1,0:T(8,128)}, u32[]{:S(2)}) copy-start(f32[1,1,2,256,256]{4,3,2,1,0:T(8,128)} %param.11) | copy-start | bytes 1572868
  7.2 194.1 %all-gather.6.cloned.1.call-start = ((), (), s32[]{:S(2)}) async-start(), calls=%async_computation.2 | async-start | bytes 4718592 | tf_op jit(solution)/shard_map/all_gather | solution.py:40
  88.6 462.2 %all-gather.4.cloned.1.call-start = ((), (), s32[]{:S(2)}) async-start(), calls=%async_computation.1 | async-start | bytes 1179648 | tf_op jit(solution)/shard_map/all_gather | solution.py:48
  90.9 580.1 %all-gather.8.cloned.1.call-start = ((), (), s32[]{:S(2)}) async-start(), calls=%async_computation.3 | async-start | bytes 4259840 | tf_op jit(solution)/shard_map/all_gather | solution.py:62
  211.0 2.0 copy-start.2
  522.3 4.7 copy-start.1
  677.5 8.8 %copy-start.5 = (s32[1,1,2]{2,1,0:T(1,128)S(1)}, s32[1,1,2]{2,1,0:T(1,128)}, u32[]{:S(2)}) copy-start(s32[1,1,2]{2,1,0:T(1,128)} %param.13) | copy-start | bytes 28
  677.5 8.9 %copy-start.4 = (s32[1,1,2]{2,1,0:T(1,128)S(1)}, s32[1,1,2]{2,1,0:T(1,128)}, u32[]{:S(2)}) copy-start(s32[1,1,2]{2,1,0:T(1,128)} %param.12) | copy-start | bytes 28
  677.5 147.9 %all-to-all-start = ((bf16[8,2048,128]{1,2,0:T(8,128)(2,1)}), bf16[8,2048,128]{1,2,0:T(8,128)(2,1)}, u32[]{:S(2)}, u32[]{:S(2)}) async-start(bf16[8,2048,128]{1,2,0:T(8,128)(2,1)} %copy.22), calls=%async_computation | async-start | bytes 8388608 | tf_op jit(solution)/shard_map/all_to_all | solution.py:63
  688.9 9.0 %copy-start.3 = (bf16[256,128]{1,0:T(8,128)(2,1)S(1)}, bf16[256,128]{1,0:T(8,128)(2,1)}, u32[]{:S(2)}) copy-start(bf16[256,128]{1,0:T(8,128)(2,1)} %get-tuple-element.73) | copy-start | bytes 196612
  689.2 136.1 %collective-permute-start = (bf16[256,2048]{1,0:T(8,128)(2,1)S(1)}, bf16[256,2048]{1,0:T(8,128)(2,1)}, u32[]{:S(2)}, u32[]{:S(2)}) collective-permute-start(bf16[256,2048]{1,0:T(8,128)(2,1)S(1)} %bitcast.139), channel_id=1, source_target_pairs={{0,256},{8,264},{16,272},{24,280},{32,288},{40,296},{48,304},{56,3... | collective-permute-start | bytes 3145736 | tf_op jit(solution)/shard_map/ppermute | solution.py:8
Sparse Core Ops, SparseCore 0:
  88.8 112.4 all-gather.5
  204.9 64.0 all-gather.3
  554.0 116.9 all-gather.7
where the time goes:
time: 849 us; the launch traced here: 838 us
  other arithmetic  265 us (31%)
  waiting for transfers between devices  225 us (27%)
  blocking collectives  208 us (24%)
  matrix products  65.5 us (8%)
  local copies, waits for them, and re-layouts  41 us (5%)
  between operations  20 us (2%)
  starting transfers between devices  14.2 us (2%)
    another operation x30, other arithmetic, body(): factor = jnp.linalg.cholesky(whole_pivot)  172 us
    all_gather x1, blocking collectives, body(): own_rows = lax.all_gather(rounded_piece, 'grp', axis=1, tiled=True)  127 us
    all_gather x1, waiting for transfers between devices, body(): every_row = lax.all_gather(rounded_piece, 'sub', axis=0, tiled=True)  117 us
    all_gather x1, waiting for transfers between devices, body(): whole_pivot = lax.all_gather(partial_value, 'grp', axis=1, tiled=True)  108 us
    another operation x3, other arithmetic, body(): jax.scipy.linalg.solve_triangular(factor, jnp.eye(width, dtype=jnp.float3...  83.6 us
    all_gather x1, blocking collectives, body(): partial_value = lax.all_gather(front_pivot, 'sub', axis=0, tiled=True)  80.4 us
    another operation x15, matrix products, body(): jax.scipy.linalg.solve_triangular(factor, jnp.eye(width, dtype=jnp.float3...  28.5 us
    another operation x14, matrix products, body(): factor = jnp.linalg.cholesky(whole_pivot)  23.1 us
  transfers between devices with their start and end apart: 5, of which 2 were waited for; matrix products, arithmetic and copies ran while one was open for 42% of the time, Pallas kernels for 0%

commit v1 on v0

v1 whole, which is shorter than its diff:
```python
import jax
import jax.numpy as jnp
from jax import lax
from jax.experimental import pallas as pl
from jax.experimental.pallas import tpu as pltpu
from jax.sharding import PartitionSpec as P

F32, BF16 = jnp.float32, jnp.bfloat16
MESH = pl.DeviceIdType.MESH
NB = 8


def row_of(v, r):
    return jnp.broadcast_to(v[r : r + 1, :], v.shape)


def lane_of(v, c):
    return jnp.broadcast_to(v[:, c : c + 1], v.shape)


def inverse_factor(block):
    strips = block.shape[0] // 8
    width = block.shape[1]
    sub = lax.broadcasted_iota(jnp.int32, (8, width), 0)
    lane = lax.broadcasted_iota(jnp.int32, (8, width), 1)
    unit = [(lane == sub + 8 * t).astype(F32) for t in range(strips)]
    left = [block[8 * t : 8 * t + 8, :] for t in range(strips)]
    out = []
    for k in range(strips):
        pivot, jordan, forward = left[k], unit[k], unit[k]
        cols = [lane_of(pivot, 8 * k + c) for c in range(8)]
        diag = jnp.ones((8, width), F32)
        for r in range(0, 8, 2):
            a = row_of(cols[r], r)
            b = row_of(cols[r], r + 1)
            d = row_of(cols[r + 1], r + 1)
            det = a * d - b * b
            over = 1.0 / det
            over_a = 1.0 / a
            ia, ib, id_ = d * over, -b * over, a * over
            is0, is1 = sub == r, sub == r + 1
            pair = is0 | is1
            g0 = jnp.where(is0, -ia, jnp.where(is1, -ib, cols[r] * ia + cols[r + 1] * ib))
            g1 = jnp.where(is0, -ib, jnp.where(is1, -id_, cols[r] * ib + cols[r + 1] * id_))
            f0, f1 = row_of(forward, r), row_of(forward, r + 1)
            forward = jnp.where(
                sub > r + 1,
                forward - g0 * f0 - g1 * f1,
                jnp.where(is1, forward - (b * over_a) * f0, forward),
            )
            diag = jnp.where(is0, a, jnp.where(is1, det * over_a, diag))

            def step(v):
                return (jnp.where(pair, 0.0, v) - g0 * row_of(v, r)) - g1 * row_of(v, r + 1)

            for c in range(r + 2, 8):
                cols[c] = step(cols[c])
            jordan, pivot = step(jordan), step(pivot)
        out.append(forward * lax.rsqrt(diag))
        prow = [row_of(pivot, c) for c in range(8)]
        jrow = [row_of(jordan, c) for c in range(8)]
        for t in range(k + 1, strips):
            coef = [lane_of(left[t], 8 * k + c) for c in range(8)]

            def total(q):
                p = [coef[c] * q[c] for c in range(8)]
                return ((p[0] + p[1]) + (p[2] + p[3])) + ((p[4] + p[5]) + (p[6] + p[7]))

            left[t] = left[t] - total(prow)
            unit[t] = unit[t] - total(jrow)
    return jnp.concatenate(out, axis=0)


def split(v):
    hi = v.astype(BF16)
    return hi, (v - hi.astype(F32)).astype(BF16)


def nt(a, b):
    return lax.dot_general(a, b, (((1,), (1,)), ((), ())), preferred_element_type=F32)


def nt3(ah, al, bh, bl):
    return nt(ah, bh) + (nt(ah, bl) + nt(al, bh))


class Chan:
    def __init__(self, send, recv):
        self.send, self.recv = send, recv

    def copy(self, src, dst, idx, device):
        return pltpu.make_async_remote_copy(
            src_ref=src, dst_ref=dst, send_sem=self.send.at[idx], recv_sem=self.recv.at[idx],
            device_id=device, device_id_type=MESH,
        )


def front_kernel(
    mask_ref, slot_ref, far_ref, trail_ref, below_ref, pivot_ref, tiles_ref,
    schur_ref, panel_ref,
    apiv, own, mine, lhi, llo, xhi, xlo, rall, cur, bcur, inv_h, inv_l, tout, tin, iout, iin,
    p1s, p1r, p2s, p2r, p3s, p3r, p4s, p4r, o1s, o1r, o2s, o2r, m1s, m1r, m2s, m2r,
    ts, tr, rs, rr, qs, qr,
):
    sub = lax.axis_index("sub")
    grp = lax.axis_index("grp")
    y, zl, core = sub // 8, (sub // 2) % 4, sub % 2
    x, zh = grp // 2, grp % 2
    z = zh * 4 + zl
    mate = 1 - core
    me = zl * 2 + core

    def at(yy, zz, cc, xx, hh):
        return ((yy * 4 + zz) * 2 + cc, xx * 2 + hh)

    def z_dev(d):
        zz = (z + d) % 8
        return at(y, zz % 4, core, x, zz // 4)

    def y_dev(d):
        return at((y + d) % 8, zl, core, x, zh)

    def x_dev(d):
        return at(y, zl, core, (x + d) % 4, zh)

    def line_dev(d):
        return at(y, (zl + d) % 4, core, x, zh)

    mate_dev = at(y, zl, mate, x, zh)
    p1, p2, p3, p4 = Chan(p1s, p1r), Chan(p2s, p2r), Chan(p3s, p3r), Chan(p4s, p4r)
    o1, o2, m1, m2 = Chan(o1s, o1r), Chan(o2s, o2r), Chan(m1s, m1r), Chan(m2s, m2r)
    tc, rc, qc = Chan(ts, tr), Chan(rs, rr), Chan(qs, qr)

    keep = mask_ref[0].astype(F32)
    apiv[grp, y, core, pl.ds(zl * 16, 16), :] = pivot_ref[...]
    own[grp] = below_ref[...] * keep
    tout[...] = tiles_ref[...].astype(BF16)
    line = lax.broadcasted_iota(jnp.int32, (8, 128), 0)
    info = jnp.zeros((8, 128), F32)
    for u in range(2):
        info = jnp.where(line == u, slot_ref[u].astype(F32), info)
        info = jnp.where(line == 2 + u, far_ref[u].astype(F32), info)
    iout[...] = info

    barrier = pltpu.get_barrier_semaphore()

    def greet(device):
        pl.semaphore_signal(barrier, inc=1, device_id=device, device_id_type=MESH)

    for d in range(1, 8):
        greet(z_dev(d))
        greet(y_dev(d))
    for d in range(1, 4):
        greet(x_dev(d))
    greet(mate_dev)
    for g in range(8):
        @pl.when((grp != g) | (y != grp))
        def _():
            greet(at(grp, zl, core, g // 2, g % 2))
    pl.semaphore_wait(barrier, 26 - (y == grp).astype(jnp.int32))

    def p1_copy(d):
        ref = apiv.at[grp, y, core, pl.ds(zl * 16, 16)]
        return p1.copy(ref, ref, d - 1, z_dev(d))

    for d in range(1, 8):
        p1_copy(d).start()

    def o1_copy():
        return o1.copy(own.at[grp], own.at[grp], 0, at(y, zl, core, x, 1 - zh))

    def m1_copy(k):
        return m1.copy(
            own.at[grp, pl.ds(32 * k, 32)], mine.at[grp, k], grp, at(k, zl, core, y // 2, y % 2)
        )

    def m1_home(k):
        return pltpu.make_async_copy(own.at[grp, pl.ds(32 * k, 32)], mine.at[grp, k], m1r.at[grp])

    def m1_self(k):
        return (y == grp) & (y == k)

    o1_copy().start()
    for k in range(8):
        @pl.when(m1_self(k))
        def _():
            m1_home(k).start()

        @pl.when(jnp.logical_not(m1_self(k)))
        def _():
            m1_copy(k).start()

    def needed(g, yy):
        return (g < 4) | (yy >= 4)

    def p2_copy(d, h, yy):
        ref = apiv.at[2 * x + h, yy, core]
        return p2.copy(ref, ref, (d - 1, h), y_dev(d))

    for d in range(1, 8):
        zz = (z + 8 - d) % 8
        ref = apiv.at[2 * x + zz // 4, y, core, pl.ds((zz % 4) * 16, 16)]
        p1.copy(ref, ref, d - 1, z_dev(d)).wait_recv()
    for h in range(2):
        for d in range(1, 8):
            @pl.when(needed(2 * x + h, y))
            def _():
                p2_copy(d, h, y).start()

    def p3_copy(d, h, v, xx):
        ref = apiv.at[2 * xx + h, pl.ds(4 * v, 4), core]
        return p3.copy(ref, ref, (d - 1, h, v), x_dev(d))

    for h in range(2):
        for v in range(2):
            @pl.when(needed(2 * x + h, 4 * v))
            def _():
                for yy in range(4 * v, 4 * v + 4):
                    @pl.when(y != yy)
                    def _():
                        d = (y + 8 - yy) % 8
                        p2_copy(d, h, yy).wait_recv()
                for d in range(1, 4):
                    p3_copy(d, h, v, x).start()

    def m2_copy(d, h, yy):
        ref = mine.at[pl.ds(4 * h, 4), yy]
        return m2.copy(ref, ref, (d - 1, h), y_dev(d))

    def o2_copy(d, xx):
        ref = own.at[pl.ds(2 * xx, 2)]
        return o2.copy(ref, ref, d - 1, x_dev(d))

    def t_copies():
        far_dev = y_dev(4)
        return (tc.copy(tout, tin, 0, far_dev), tc.copy(iout, iin, 1, far_dev))

    def start_rows():
        o1.copy(own.at[grp], own.at[x * 2 + 1 - zh], 0, at(y, zl, core, x, 1 - zh)).wait_recv()
        for d in range(1, 4):
            o2_copy(d, x).start()
        for g in range(8):
            m1.copy(own.at[0, pl.ds(0, 32)], mine.at[g, y], g, mate_dev).wait_recv()
        for h in range(2):
            for d in range(1, 8):
                m2_copy(d, h, y).start()

    def p4_copy(g, half):
        ref = apiv.at[g, :, half]
        return p4.copy(ref, ref, g, mate_dev)

    def forward(g):
        d = (x + 4 - g // 2) % 4

        @pl.when(d != 0)
        def _():
            for v in range(2):
                @pl.when(needed(g, 4 * v))
                def _():
                    p3_copy(d, g % 2, v, g // 2).wait_recv()

        p4_copy(g, core).start()

    def arrived(g):
        p4_copy(g, mate).wait_recv()

    def column(g):
        return apiv[g].reshape(8, 2, 4, 16, 128).swapaxes(1, 2).reshape(1024, 128)

    def r_copy(d, j, who):
        ref = rall.at[j, who]
        return rc.copy(ref, ref, (d - 1, j), line_dev(d))

    def q_copy(i, j, who):
        ref = rall.at[j, who]
        return qc.copy(ref, ref, (i, j), mate_dev)

    def line_row(d, cc):
        return ((zl + 4 - d) % 4) * 2 + cc

    def send_rows(j):
        for d in range(1, 4):
            r_copy(d, j, me).start()
        q_copy(0, j, me).start()

    def pass_rows(j):
        for d in range(1, 4):
            r_copy(d, j, line_row(d, core)).wait_recv()
            q_copy(d, j, line_row(d, core)).start()

    def rows_arrived(j):
        for d in range(4):
            q_copy(d, j, line_row(d, mate)).wait_recv()

    def solve_rows(j):
        at_j = pl.ds(pl.multiple_of(j * 128, 128), 128)
        rest = bcur[...] - nt3(xhi[...], xlo[...], lhi[at_j, :], llo[at_j, :])
        rh, rl = split(rest)
        return nt3(rh, rl, inv_h[...], inv_l[...])

    def keep_rows(j, sol):
        at_j = pl.ds(pl.multiple_of(j * 128, 128), 128)
        sh, sl = split(sol)
        xhi[:, at_j] = sh
        xlo[:, at_j] = sl
        rall[j, me] = sh[256:]

        @pl.when(grp == j)
        def _():
            panel_ref[...] = sol[:256]

        send_rows(j)

    def take_rows(j):
        @pl.when(j % 2 == 0)
        def _():
            d = (x + 4 - j // 2) % 4

            @pl.when(d != 0)
            def _():
                o2_copy(d, j // 2).wait_recv()

        for h in range(2):
            @pl.when(j == 4 * h)
            def _():
                for d in range(1, 8):
                    m2_copy(d, h, (y + 8 - d) % 8).wait_recv()

        bcur[:256, :] = own[j]
        bcur[256:, :] = mine[j].reshape(256, 128)

    zero = jnp.zeros((1024, 1024), BF16)
    lhi[...] = zero
    llo[...] = zero
    xhi[...] = jnp.zeros((512, 1024), BF16)
    xlo[...] = jnp.zeros((512, 1024), BF16)
    bcur[...] = jnp.zeros((512, 128), F32)
    inv_h[...] = jnp.zeros((128, 128), BF16)
    inv_l[...] = jnp.zeros((128, 128), BF16)
    rows = lax.broadcasted_iota(jnp.int32, (1024, 128), 0)

    forward(0)
    start_rows()
    forward(1)
    arrived(0)
    cur[...] = column(0)

    def step(j, _):
        nxt = jnp.minimum(j + 1, 7)
        at_j = pl.ds(pl.multiple_of(j * 128, 128), 128)
        at_n = pl.ds(pl.multiple_of(nxt * 128, 128), 128)
        inv = inverse_factor(cur[at_j, :])
        past = nt3(lhi[...], llo[...], lhi[at_n, :], llo[at_n, :])
        sol = solve_rows(jnp.maximum(j - 1, 0))

        @pl.when(j >= 1)
        def _():
            keep_rows(j - 1, sol)

        @pl.when(j == 2)
        def _():
            for copy in t_copies():
                copy.start()

        @pl.when(j >= 2)
        def _():
            pass_rows(j - 2)

        @pl.when(j < 6)
        def _():
            forward(j + 2)

        take_rows(j)

        @pl.when(j < 7)
        def _():
            arrived(j + 1)

        ih, il = split(inv)
        inv_h[...] = ih
        inv_l[...] = il

        @pl.when(j < 7)
        def _():
            ch, cl = split(cur[...])
            low = jnp.where(rows >= (j + 1) * 128, nt3(ch, cl, ih, il), 0.0)
            lh, ll = split(low)
            lhi[:, at_j] = lh
            llo[:, at_j] = ll
            cur[...] = (column(nxt) - past) - nt3(lh, ll, lhi[at_n, at_j], llo[at_n, at_j])

        return 0

    lax.fori_loop(0, 8, step, 0)
    keep_rows(7, solve_rows(7))
    pass_rows(6)

    for copy in t_copies():
        copy.wait_recv()
    for j in range(7):
        rows_arrived(j)

    def weight(slots, flags, u, q, want):
        s, f = slots[u : u + 1, 0:1], flags[u : u + 1, 0:1]
        return jnp.where((s == q) & (f == want), 1.0, 0.0)

    def product(q, j0, j1):
        other = [rall[j, q] for j in range(j0, j1)]
        other = other[0] if len(other) == 1 else jnp.concatenate(other, axis=1)
        return nt(xhi[:256, 128 * j0 : 128 * j1], other)

    def first(q, _):
        qf = q.astype(F32)
        cols = pl.ds(pl.multiple_of(q * 256, 256), 256)
        near_s, near_f = iout[0:2, :], iout[2:4, :]
        far_s, far_f = iin[0:2, :], iin[2:4, :]
        acc = trail_ref[:, cols] - product(q, 0, 7)
        for u in range(2):
            acc = acc + weight(near_s, near_f, u, qf, 0.0) * tiles_ref[u]
            acc = acc + weight(far_s, far_f, u, qf, 1.0) * tin[u].astype(F32)
        schur_ref[:, cols] = acc
        return 0

    lax.fori_loop(0, 8, first, 0)
    pass_rows(7)
    rows_arrived(7)

    def second(q, _):
        cols = pl.ds(pl.multiple_of(q * 256, 256), 256)
        schur_ref[:, cols] = schur_ref[:, cols] - product(q, 7, 8)
        return 0

    lax.fori_loop(0, 8, second, 0)

    for d in range(1, 8):
        p1_copy(d).wait_send()
        for h in range(2):
            m2_copy(d, h, y).wait_send()

            @pl.when(needed(2 * x + h, y))
            def _():
                p2_copy(d, h, y).wait_send()
    for d in range(1, 4):
        o2_copy(d, x).wait_send()
        for h in range(2):
            for v in range(2):
                @pl.when(needed(2 * x + h, 4 * v))
                def _():
                    p3_copy(d, h, v, x).wait_send()
    o1_copy().wait_send()
    for k in range(8):
        @pl.when(jnp.logical_not(m1_self(k)))
        def _():
            m1_copy(k).wait_send()
    for copy in t_copies():
        copy.wait_send()

    def sent(j, _):
        p4_copy(j, core).wait_send()
        for d in range(1, 4):
            r_copy(d, j, me).wait_send()
            q_copy(d, j, line_row(d, core)).wait_send()
        q_copy(0, j, me).wait_send()
        return 0

    lax.fori_loop(0, 8, sent, 0)


def body(front_trail, front_below, front_pivot, panel_mask, child_tiles, child_slot, child_far):
    smem = pl.BlockSpec(memory_space=pltpu.SMEM)
    vmem = pl.BlockSpec(memory_space=pltpu.VMEM)
    dma = pltpu.SemaphoreType.DMA
    pairs = [(7,), (7, 2), (3, 2, 2), (8,), (1,), (3,), (8,), (7, 2), (2,), (3, 8), (4, 8)]
    return pl.pallas_call(
        front_kernel,
        in_specs=[smem] * 3 + [vmem] * 4,
        out_specs=[vmem, vmem],
        out_shape=[
            jax.ShapeDtypeStruct(front_trail.shape, F32),
            jax.ShapeDtypeStruct(front_below.shape, F32),
        ],
        scratch_shapes=[
            pltpu.VMEM((8, 8, 2, 64, 128), F32),
            pltpu.VMEM((8, 256, 128), F32),
            pltpu.VMEM((8, 8, 32, 128), F32),
            pltpu.VMEM((1024, 1024), BF16),
            pltpu.VMEM((1024, 1024), BF16),
            pltpu.VMEM((512, 1024), BF16),
            pltpu.VMEM((512, 1024), BF16),
            pltpu.VMEM((8, 8, 256, 128), BF16),
            pltpu.VMEM((1024, 128), F32),
            pltpu.VMEM((512, 128), F32),
            pltpu.VMEM((128, 128), BF16),
            pltpu.VMEM((128, 128), BF16),
            pltpu.VMEM((2, 256, 256), BF16),
            pltpu.VMEM((2, 256, 256), BF16),
            pltpu.VMEM((8, 128), F32),
            pltpu.VMEM((8, 128), F32),
        ]
        + [dma(shape) for shape in pairs for _ in range(2)],
        compiler_params=pltpu.CompilerParams(
            collective_id=0, has_side_effects=True, vmem_limit_bytes=60 * 2**20
        ),
        cost_estimate=pl.CostEstimate(
            flops=6_000_000_000, bytes_accessed=6_000_000, transcendentals=0
        ),
        name="front",
    )(
        panel_mask,
        child_slot.reshape(2),
        child_far.reshape(2),
        front_trail,
        front_below,
        front_pivot,
        child_tiles.reshape(2, 256, 256),
    )


def solution(mesh):
    return jax.shard_map(
        body,
        mesh=mesh,
        in_specs=(
            P("sub", "grp"),
            P("sub", "grp"),
            P("sub", "grp"),
            P("sub"),
            P("sub", "grp", None, None, None),
            P("sub", "grp", None),
            P("sub", "grp", None),
        ),
        out_specs=(P("sub", "grp"), P("sub", "grp")),
        check_vma=False,
    )
```

time: 849 us -> 134 us (0.16)
  the two profiles are of different devices: /device:TPU:64 before, /device:TPU:70 now
where the time goes in v1:
time: 134 us
  Pallas kernels  129 us (96%)
  local copies, waits for them, and re-layouts  3.83 us (3%)
    pallas_call x1, Pallas kernels, body(): pl.pallas_call(front_kernel, in_specs=[smem] * 3 + [vmem] * 4, out_specs=...  129 us
    unnamed x4, local copies, waits for them, and re-layouts  3.83 us

profile of v1, /device:TPU:70, one launch (start us, length us, event | category | flops | bytes accessed | tf_op | source)
XLA Modules:
  0.0 134.3 jit_solution(6062061811832082146)
XLA Ops:
  1.3 129.2 %front.1 = (f32[256,2048]{1,0:T(8,128)}, f32[256,128]{1,0:T(8,128)}) custom-call(s32[1]{0:T(128)S(6)} %copy.11.mask_ref, s32[2]{0:T(128)} %bitcast.4, s32[2]{0:T(128)} %bitcast.5, f32[256,2048]{1,0:T(8,128)} %trail_ref.1, f32[256,128]{1,0:T(8,128)} %below_ref.1, f32[16,128]{1,0:T(8,128)} %pivot_ref.1, f32[2,256,256]{2,1,0:T(8,128)} %bitcast.3), custom_call_target="tpu_custom_call" | custom-call | flops 6000000000 | bytes 6000000 | tf_op jit(solution)/shard_map/front/pallas_call | solution.py:474
  130.5 0.0 copy-start
  130.5 3.2 %copy.12 = f32[256,2048]{1,0:T(8,128)} copy(f32[256,2048]{1,0:T(8,128)} %get-tuple-element.4) | data formatting | bytes 4194304
  133.6 0.0 copy-done
  133.6 0.7 copy.13
Async XLA Ops:
  130.5 3.2 %copy-start = (f32[256,128]{1,0:T(8,128)S(1)}, f32[256,128]{1,0:T(8,128)}, u32[]{:S(2)}) copy-start(f32[256,128]{1,0:T(8,128)} %get-tuple-element.5) | copy-start | bytes 393220

commit v2 on v1

v2 whole, which is shorter than its diff:
```python
import jax
import jax.numpy as jnp
from jax import lax
from jax.experimental import pallas as pl
from jax.experimental.pallas import tpu as pltpu
from jax.sharding import PartitionSpec as P

F32, BF16 = jnp.float32, jnp.bfloat16
MESH = pl.DeviceIdType.MESH
NB = 8


def row_of(v, r):
    return jnp.broadcast_to(v[r : r + 1, :], v.shape)


def lane_of(v, c):
    return jnp.broadcast_to(v[:, c : c + 1], v.shape)


def inverse_factor(block):
    strips = block.shape[0] // 8
    width = block.shape[1]
    sub = lax.broadcasted_iota(jnp.int32, (8, width), 0)
    lane = lax.broadcasted_iota(jnp.int32, (8, width), 1)
    unit = [(lane == sub + 8 * t).astype(F32) for t in range(strips)]
    left = [block[8 * t : 8 * t + 8, :] for t in range(strips)]
    out = []
    for k in range(strips):
        pivot, jordan, forward = left[k], unit[k], unit[k]
        cols = [lane_of(pivot, 8 * k + c) for c in range(8)]
        diag = jnp.ones((8, width), F32)
        for r in range(0, 8, 2):
            a = row_of(cols[r], r)
            b = row_of(cols[r], r + 1)
            d = row_of(cols[r + 1], r + 1)
            det = a * d - b * b
            over = 1.0 / det
            over_a = 1.0 / a
            ia, ib, id_ = d * over, -b * over, a * over
            is0, is1 = sub == r, sub == r + 1
            pair = is0 | is1
            g0 = jnp.where(is0, -ia, jnp.where(is1, -ib, cols[r] * ia + cols[r + 1] * ib))
            g1 = jnp.where(is0, -ib, jnp.where(is1, -id_, cols[r] * ib + cols[r + 1] * id_))
            f0, f1 = row_of(forward, r), row_of(forward, r + 1)
            forward = jnp.where(
                sub > r + 1,
                forward - g0 * f0 - g1 * f1,
                jnp.where(is1, forward - (b * over_a) * f0, forward),
            )
            diag = jnp.where(is0, a, jnp.where(is1, det * over_a, diag))

            def step(v):
                return (jnp.where(pair, 0.0, v) - g0 * row_of(v, r)) - g1 * row_of(v, r + 1)

            for c in range(r + 2, 8):
                cols[c] = step(cols[c])
            jordan, pivot = step(jordan), step(pivot)
        out.append(forward * lax.rsqrt(diag))
        prow = [row_of(pivot, c) for c in range(8)]
        jrow = [row_of(jordan, c) for c in range(8)]
        for t in range(k + 1, strips):
            coef = [lane_of(left[t], 8 * k + c) for c in range(8)]

            def total(q):
                p = [coef[c] * q[c] for c in range(8)]
                return ((p[0] + p[1]) + (p[2] + p[3])) + ((p[4] + p[5]) + (p[6] + p[7]))

            left[t] = left[t] - total(prow)
            unit[t] = unit[t] - total(jrow)
    return jnp.concatenate(out, axis=0)


def split(v):
    hi = v.astype(BF16)
    return hi, (v - hi.astype(F32)).astype(BF16)


def nt(a, b):
    return lax.dot_general(a, b, (((1,), (1,)), ((), ())), preferred_element_type=F32)


def nt3(ah, al, bh, bl):
    return nt(ah, bh) + (nt(ah, bl) + nt(al, bh))


class Chan:
    def __init__(self, send, recv):
        self.send, self.recv = send, recv

    def copy(self, src, dst, idx, device):
        return pltpu.make_async_remote_copy(
            src_ref=src, dst_ref=dst, send_sem=self.send.at[idx], recv_sem=self.recv.at[idx],
            device_id=device, device_id_type=MESH,
        )


def front_kernel(
    mask_ref, slot_ref, far_ref, below_ref, pivot_ref, tiles_ref,
    delta_ref, panel_ref,
    apiv, kept, own, mine, lhi, llo, xhi, xlo, rall, cur, diag, bcur, inv_h, inv_l, tout, tin, iout, iin, acc,
    p1s, p1r, p2s, p2r, p3s, p3r, p4s, p4r, o1s, o1r, o2s, o2r, m1s, m1r, m2s, m2r,
    ts, tr, rs, rr, us, ur, qs, qr, out_sem, home_sem,
):
    sub = lax.axis_index("sub")
    grp = lax.axis_index("grp")
    y, zl, core = sub // 8, (sub // 2) % 4, sub % 2
    x, zh = grp // 2, grp % 2
    z = zh * 4 + zl
    mate = 1 - core

    def at(yy, zz, cc, xx, hh):
        return ((yy * 4 + zz) * 2 + cc, xx * 2 + hh)

    def y_dev(d):
        return at((y + d) % 8, zl, core, x, zh)

    def x_dev(d):
        return at(y, zl, core, (x + d) % 4, zh)

    def grp_dev(d):
        g = (grp + d) % 8
        return at(y, zl, core, g // 2, g % 2)

    def line_dev(d):
        return at(y, (zl + d) % 4, core, x, zh)

    mate_dev = at(y, zl, mate, x, zh)
    p1, p2, p3, p4 = Chan(p1s, p1r), Chan(p2s, p2r), Chan(p3s, p3r), Chan(p4s, p4r)
    o1, o2, m1, m2 = Chan(o1s, o1r), Chan(o2s, o2r), Chan(m1s, m1r), Chan(m2s, m2r)
    tc, rc, uc, qc = Chan(ts, tr), Chan(rs, rr), Chan(us, ur), Chan(qs, qr)

    barrier = pltpu.get_barrier_semaphore()

    def greet(device):
        pl.semaphore_signal(barrier, inc=1, device_id=device, device_id_type=MESH)

    for d in range(1, 8):
        greet(y_dev(d))
    for d in range(1, 4):
        greet(line_dev(d))
    for d in range(1, 8):
        greet(grp_dev(d))
    for g in range(8):
        @pl.when((g != grp) | (x != zl))
        def _():
            greet(at(y, x, core, g // 2, g % 2))
    greet(mate_dev)
    for g in range(8):
        @pl.when((grp != g) | (y != grp))
        def _():
            greet(at(grp, zl, core, g // 2, g % 2))

    keep = mask_ref[0].astype(F32)
    kept[...] = below_ref[...] * keep
    tout[...] = tiles_ref[...].astype(BF16)
    line = lax.broadcasted_iota(jnp.int32, (8, 128), 0)
    info = jnp.zeros((8, 128), F32)
    for u in range(2):
        info = jnp.where(line == u, slot_ref[u].astype(F32), info)
        info = jnp.where(line == 2 + u, far_ref[u].astype(F32), info)
    iout[...] = info

    zero = jnp.zeros((1024, 1024), BF16)
    lhi[...] = zero
    llo[...] = zero
    xhi[...] = jnp.zeros((384, 1024), BF16)
    xlo[...] = jnp.zeros((384, 1024), BF16)
    cur[...] = jnp.zeros((1024, 128), F32)
    bcur[...] = jnp.zeros((384, 128), F32)
    inv_h[...] = jnp.zeros((8, 128, 128), BF16)
    inv_l[...] = jnp.zeros((8, 128, 128), BF16)
    pl.semaphore_wait(
        barrier, 34 - (y == grp).astype(jnp.int32) - (x == zl).astype(jnp.int32)
    )

    def p1_copy(zz):
        return p1.copy(
            pivot_ref, apiv.at[grp, y, core, zl], grp, at(y, zz % 4, core, zl, zz // 4)
        )

    def p1_self(zz):
        return (x == zl) & (z == zz)

    def p1_home():
        return pltpu.make_async_copy(pivot_ref, apiv.at[grp, y, core, zl], p1r.at[grp])

    for zz in range(8):
        @pl.when(jnp.logical_not(p1_self(zz)))
        def _():
            p1_copy(zz).start()

    @pl.when(x == zl)
    def _():
        p1_home().start()

    spans = ((0, 1, 0), (1, 1, 1), (2, 2, 2), (4, 4, 4))

    def p2_copy(d, i, yy):
        ref = apiv.at[pl.ds(*spans[i][:2]), yy, core, x]
        return p2.copy(ref, ref, (d - 1, i), y_dev(d))

    for g in range(8):
        p1.copy(pivot_ref, apiv.at[g, y, core, x], g, mate_dev).wait_recv()
    for i in range(4):
        @pl.when(y >= spans[i][2])
        def _():
            for d in range(1, 8):
                p2_copy(d, i, y).start()

    def o1_copy(d):
        quarter = ((grp + d) % 8) // 2
        return o1.copy(
            kept.at[pl.ds(64 * quarter, 64)], own.at[grp, quarter], d - 1, grp_dev(d)
        )

    def o1_home():
        return pltpu.make_async_copy(kept.at[pl.ds(64 * x, 64)], own.at[grp, x], home_sem)

    def m1_copy(k):
        return m1.copy(
            kept.at[pl.ds(32 * k, 32)], mine.at[grp, k // 2], grp, at(k, zl, core, y // 2, y % 2)
        )

    def m1_home(k):
        return pltpu.make_async_copy(
            kept.at[pl.ds(32 * k, 32)], mine.at[grp, k // 2], m1r.at[grp]
        )

    def m1_self(k):
        return (y == grp) & (y == k)

    for d in range(1, 8):
        o1_copy(d).start()
    o1_home().start()
    for k in range(8):
        @pl.when(m1_self(k))
        def _():
            m1_home(k).start()

        @pl.when(jnp.logical_not(m1_self(k)))
        def _():
            m1_copy(k).start()

    items = ((0, 0, 1), (0, 1, 7), (1, 1, 7), (2, 2, 6), (3, 4, 4))

    def p3_copy(d, i, xx):
        span, first, count = items[i]
        ref = apiv.at[pl.ds(*spans[span][:2]), pl.ds(first, count), core, xx]
        return p3.copy(ref, ref, (d - 1, i), x_dev(d))

    def spread(i):
        span, first, count = items[i]
        for yy in range(first, first + count):
            @pl.when(y != yy)
            def _():
                p2_copy((y + 8 - yy) % 8, span, yy).wait_recv()
        for d in range(1, 4):
            p3_copy(d, i, x).start()

    groups = ((0, 2), (2, 3), (5, 3))

    def m2_copy(d, h, yy):
        ref = mine.at[pl.ds(*groups[h]), yy // 2]
        return m2.copy(ref, ref, (d - 1, h), y_dev(2 * d))

    def o2_copy(d, h, xx):
        ref = own.at[pl.ds(*groups[h]), xx]
        return o2.copy(ref, ref, (d - 1, h), x_dev(d))

    def t_copies():
        far_dev = y_dev(4)
        return (tc.copy(tout, tin, 0, far_dev), tc.copy(iout, iin, 1, far_dev))

    def rows_here():
        o1_home().wait()
        for d in range(1, 8):
            o1.copy(
                kept.at[pl.ds(0, 64)], own.at[(grp + 8 - d) % 8, x], d - 1, grp_dev(d)
            ).wait_recv()
        for g in range(8):
            m1.copy(kept.at[pl.ds(0, 32)], mine.at[g, y // 2], g, mate_dev).wait_recv()

    def start_rows(h):
        for d in range(1, 4):
            m2_copy(d, h, y).start()
            o2_copy(d, h, x).start()

    def p4_copy(i, half):
        span, first, count = items[i]
        ref = apiv.at[pl.ds(*spans[span][:2]), pl.ds(first, count), half]
        return p4.copy(ref, ref, i, mate_dev)

    def forward(i):
        for d in range(1, 4):
            p3_copy(d, i, (x + 4 - d) % 4).wait_recv()
        p4_copy(i, core).start()

    def arrived(i):
        p4_copy(i, mate).wait_recv()

    def natural(v):
        n = v.shape[0]
        return v.swapaxes(1, 2).reshape(n * 128, 128)

    def column(g):
        return natural(apiv[g])

    def diagonal(g):
        return natural(apiv[g, pl.ds(g, 1)])

    side = y % 2

    def r_copy(d, j, row):
        ref = rall.at[j, core, side, row]
        return rc.copy(ref, ref, (d - 1, j), line_dev(d))

    def u_copy(i, j, par):
        ref = rall.at[j, core, par, pl.ds(2 * i, 2)]
        return uc.copy(ref, ref, (i, j), y_dev((1, 7)[i]))

    def q_copy(i, j, par, half):
        ref = rall.at[j, half, par]
        return qc.copy(ref, ref, (i, j), mate_dev)

    def send_rows(j):
        for d in range(1, 4):
            r_copy(d, j, zl).start()

    def pass_rows(j):
        for d in range(1, 4):
            r_copy(d, j, (zl + 4 - d) % 4).wait_recv()
        for i in range(2):
            u_copy(i, j, side).start()
        q_copy(0, j, side, core).start()

    def pass_more(j):
        for i in range(2):
            u_copy(i, j, 1 - side).wait_recv()
        q_copy(1, j, 1 - side, core).start()

    def rows_arrived(j):
        q_copy(0, j, side, mate).wait_recv()
        q_copy(1, j, 1 - side, mate).wait_recv()

    def solve_rows(j):
        at_j = pl.ds(pl.multiple_of(j * 128, 128), 128)
        rest = bcur[...] - nt3(xhi[...], xlo[...], lhi[at_j, :], llo[at_j, :])
        rh, rl = split(rest)
        return nt3(rh, rl, inv_h[j], inv_l[j])

    def keep_rows(j, sol):
        at_j = pl.ds(pl.multiple_of(j * 128, 128), 128)
        sh, sl = split(sol)
        xhi[:, at_j] = sh
        xlo[:, at_j] = sl
        rall[j, core, side, zl] = sh[256:].reshape(4, 32, 128)

        @pl.when(grp == j)
        def _():
            panel_ref[...] = sol[:256]

        send_rows(j)

    def take_rows(j):
        for h in range(3):
            @pl.when(j == groups[h][0])
            def _():
                for d in range(1, 4):
                    m2_copy(d, h, (y + 8 - 2 * d) % 8).wait_recv()
                    o2_copy(d, h, (x + 4 - d) % 4).wait_recv()

        bcur[:256, :] = own[j].reshape(256, 128)
        bcur[256:, :] = mine[j].reshape(128, 128)

    rows = lax.broadcasted_iota(jnp.int32, (1024, 128), 0)

    for i in range(3):
        spread(i)
    forward(0)
    spread(3)
    arrived(0)
    diag[...] = diagonal(0)

    def step(j, _):
        last = jnp.maximum(j - 1, 0)
        nxt = jnp.minimum(j + 1, 7)
        at_l = pl.ds(pl.multiple_of(last * 128, 128), 128)
        at_j = pl.ds(pl.multiple_of(j * 128, 128), 128)
        at_n = pl.ds(pl.multiple_of(nxt * 128, 128), 128)
        inv = inverse_factor(diag[...])
        ch, cl = split(cur[...])
        low = jnp.where(rows >= j * 128, nt3(ch, cl, inv_h[last], inv_l[last]), 0.0)
        lh, ll = split(low)
        lhi[:, at_l] = lh
        llo[:, at_l] = ll
        past = nt3(lhi[...], llo[...], lhi[at_j, :], llo[at_j, :])
        past_n = nt3(lhi[at_n, :], llo[at_n, :], lhi[at_n, :], llo[at_n, :])
        done = jnp.where(j > 4, j - 1, jnp.maximum(j - 2, 0))
        sol = solve_rows(done)

        @pl.when(j >= 2)
        def _():
            keep_rows(done, sol)

        @pl.when(j == 0)
        def _():
            forward(1)
            forward(2)
            rows_here()
            start_rows(0)
            spread(4)
            arrived(1)
            arrived(2)

        @pl.when(j == 1)
        def _():
            forward(3)
            start_rows(1)
            start_rows(2)
            arrived(3)

        @pl.when(j == 2)
        def _():
            forward(4)

        @pl.when(j == 3)
        def _():
            arrived(4)

        ih, il = split(inv)
        inv_h[j] = ih
        inv_l[j] = il
        cur[...] = column(j) - past

        @pl.when(j < 7)
        def _():
            th, tl = split(cur[at_n, :])
            nh, nl = split(nt3(th, tl, ih, il))
            diag[...] = (diagonal(nxt) - past_n) - nt3(nh, nl, nh, nl)

        @pl.when(j == 3)
        def _():
            for copy in t_copies():
                copy.start()

        @pl.when((j >= 1) & (j < 5))
        def _():
            take_rows(j - 1)

        @pl.when(j == 4)
        def _():
            keep_rows(3, solve_rows(3))

        @pl.when(j >= 4)
        def _():
            take_rows(j)

        return 0

    def pass_at(j):
        @pl.when((j >= 3) & (j < 5))
        def _():
            pass_rows(j - 3)

        @pl.when(j == 4)
        def _():
            pass_more(0)

        @pl.when(j == 5)
        def _():
            pass_rows(2)
            pass_rows(3)
            pass_more(1)

        @pl.when(j == 6)
        def _():
            pass_rows(4)
            pass_more(2)
            pass_more(3)

        @pl.when(j == 7)
        def _():
            pass_rows(5)
            pass_more(4)

    def step_and_pass(j, _):
        step(j, 0)
        pass_at(j)
        return 0

    lax.fori_loop(0, 8, step_and_pass, 0)
    keep_rows(7, solve_rows(7))
    pass_rows(6)
    pass_more(5)

    for copy in t_copies():
        copy.wait_recv()
    for j in range(6):
        rows_arrived(j)

    def weight(slots, flags, u, q, want):
        s, f = slots[u : u + 1, 0:1], flags[u : u + 1, 0:1]
        return jnp.where((s == q) & (f == want), 1.0, 0.0)

    def product(q, j0, j1):
        zq, cq = q // 2, q % 2
        other = [rall[j, cq, :, zq].swapaxes(0, 1).reshape(256, 128) for j in range(j0, j1)]
        other = other[0] if len(other) == 1 else jnp.concatenate(other, axis=1)
        return nt(xhi[:256, 128 * j0 : 128 * j1], other)

    def first(q, _):
        qf = q.astype(F32)
        cols = pl.ds(pl.multiple_of(q * 256, 256), 256)
        near_s, near_f = iout[0:2, :], iout[2:4, :]
        far_s, far_f = iin[0:2, :], iin[2:4, :]
        total = -product(q, 0, 6)
        for u in range(2):
            total = total + weight(near_s, near_f, u, qf, 0.0) * tiles_ref[u]
            total = total + weight(far_s, far_f, u, qf, 1.0) * tin[u].astype(F32)
        acc[:, cols] = total
        return 0

    lax.fori_loop(0, 8, first, 0)
    pass_more(6)
    pass_rows(7)
    for zz in range(8):
        @pl.when(jnp.logical_not(p1_self(zz)))
        def _():
            p1_copy(zz).wait_send()
    for d in range(1, 4):
        for h in range(3):
            m2_copy(d, h, y).wait_send()
            o2_copy(d, h, x).wait_send()
    for i in range(4):
        @pl.when(y >= spans[i][2])
        def _():
            for d in range(1, 8):
                p2_copy(d, i, y).wait_send()
    for i in range(5):
        p4_copy(i, core).wait_send()
        for d in range(1, 4):
            p3_copy(d, i, x).wait_send()
    for d in range(1, 8):
        o1_copy(d).wait_send()
    for k in range(8):
        @pl.when(jnp.logical_not(m1_self(k)))
        def _():
            m1_copy(k).wait_send()
    for copy in t_copies():
        copy.wait_send()

    def sent(j, _):
        for d in range(1, 4):
            r_copy(d, j, zl).wait_send()
        for i in range(2):
            u_copy(i, j, side).wait_send()
        q_copy(0, j, side, core).wait_send()
        q_copy(1, j, 1 - side, core).wait_send()
        return 0

    lax.fori_loop(0, 7, sent, 0)
    pass_more(7)
    rows_arrived(6)
    rows_arrived(7)

    def out_copy(q):
        cols = pl.ds(pl.multiple_of(q * 256, 256), 256)
        return pltpu.make_async_copy(acc.at[:, cols], delta_ref.at[:, cols], out_sem.at[q])

    def second(q, _):
        cols = pl.ds(pl.multiple_of(q * 256, 256), 256)
        acc[:, cols] = acc[:, cols] - product(q, 6, 8)
        out_copy(q).start()
        return 0

    lax.fori_loop(0, 8, second, 0)
    sent(7, 0)
    for q in range(8):
        out_copy(q).wait()


def body(front_trail, front_below, front_pivot, panel_mask, child_tiles, child_slot, child_far):
    smem = pl.BlockSpec(memory_space=pltpu.SMEM)
    vmem = pl.BlockSpec(memory_space=pltpu.VMEM)
    dma = pltpu.SemaphoreType.DMA
    pairs = [(8,), (7, 4), (3, 5), (5,), (7,), (3, 3), (8,), (3, 3), (2,), (3, 8), (2, 8), (2, 8)]
    delta, panel = pl.pallas_call(
        front_kernel,
        in_specs=[smem] * 3 + [vmem] * 3,
        out_specs=[pl.BlockSpec(memory_space=pl.ANY), vmem],
        out_shape=[
            jax.ShapeDtypeStruct(front_trail.shape, F32),
            jax.ShapeDtypeStruct(front_below.shape, F32),
        ],
        scratch_shapes=[
            pltpu.VMEM((8, 8, 2, 4, 16, 128), F32),
            pltpu.VMEM((256, 128), F32),
            pltpu.VMEM((8, 4, 64, 128), F32),
            pltpu.VMEM((8, 4, 32, 128), F32),
            pltpu.VMEM((1024, 1024), BF16),
            pltpu.VMEM((1024, 1024), BF16),
            pltpu.VMEM((384, 1024), BF16),
            pltpu.VMEM((384, 1024), BF16),
            pltpu.VMEM((8, 2, 2, 4, 4, 32, 128), BF16),
            pltpu.VMEM((1024, 128), F32),
            pltpu.VMEM((128, 128), F32),
            pltpu.VMEM((384, 128), F32),
            pltpu.VMEM((8, 128, 128), BF16),
            pltpu.VMEM((8, 128, 128), BF16),
            pltpu.VMEM((2, 256, 256), BF16),
            pltpu.VMEM((2, 256, 256), BF16),
            pltpu.VMEM((8, 128), F32),
            pltpu.VMEM((8, 128), F32),
            pltpu.VMEM((256, 2048), F32),
        ]
        + [dma(shape) for shape in pairs for _ in range(2)]
        + [dma((8,)), dma],
        compiler_params=pltpu.CompilerParams(
            collective_id=0, has_side_effects=True, vmem_limit_bytes=60 * 2**20
        ),
        cost_estimate=pl.CostEstimate(
            flops=6_000_000_000, bytes_accessed=6_000_000, transcendentals=0
        ),
        name="front",
    )(
        panel_mask,
        child_slot.reshape(2),
        child_far.reshape(2),
        front_below,
        front_pivot,
        child_tiles.reshape(2, 256, 256),
    )
    return front_trail + delta, panel


def solution(mesh):
    return jax.shard_map(
        body,
        mesh=mesh,
        in_specs=(
            P("sub", "grp"),
            P("sub", "grp"),
            P("sub", "grp"),
            P("sub"),
            P("sub", "grp", None, None, None),
            P("sub", "grp", None),
            P("sub", "grp", None),
        ),
        out_specs=(P("sub", "grp"), P("sub", "grp")),
        check_vma=False,
    )
```

time: 134 us -> 111 us (0.83)
  the two profiles are of different devices: /device:TPU:70 before, /device:TPU:5 now
where the time goes in v2:
time: 111 us
  Pallas kernels  106 us (95%)
  other arithmetic  3.28 us (3%)
  between operations  1.31 us (1%)
    pallas_call x1, Pallas kernels, body(): pl.pallas_call(front_kernel, in_specs=[smem] * 3 + [vmem] * 3, out_specs=...  106 us
    add x1, other arithmetic, body(): return (front_trail + delta, panel)  3.28 us

profile of v2, /device:TPU:5, one launch (start us, length us, event | category | flops | bytes accessed | tf_op | source)
XLA Modules:
  0.0 111.3 jit_solution(15629413632319607058)
XLA Ops:
  1.3 0.0 copy-start
  1.3 106.0 %front.1 = (f32[256,2048]{1,0:T(8,128)}, f32[256,128]{1,0:T(8,128)}) custom-call(s32[1]{0:T(128)S(6)} %copy.10.mask_ref, s32[2]{0:T(128)} %bitcast.4, s32[2]{0:T(128)} %bitcast.5, f32[256,128]{1,0:T(8,128)} %below_ref.1, f32[16,128]{1,0:T(8,128)} %pivot_ref.1, f32[2,256,256]{2,1,0:T(8,128)} %bitcast.3), custom_call_target="tpu_custom_call" | custom-call | flops 6000000000 | bytes 6000000 | tf_op jit(solution)/shard_map/front/pallas_call | solution.py:588
  107.3 0.0 copy-done
  107.3 0.0 copy-start.1
  107.3 3.3 %add.3 = f32[256,2048]{1,0:T(8,128)} add(f32[256,2048]{1,0:T(8,128)S(1)} %copy-done, f32[256,2048]{1,0:T(8,128)} %get-tuple-element.4) | non-fusion elementwise | flops 524288 | bytes 6291456 | tf_op jit(solution)/shard_map/add | solution.py:634
  110.6 0.0 copy-done.1
  110.6 0.7 copy.11
Async XLA Ops:
  1.3 106.0 %copy-start = (f32[256,2048]{1,0:T(8,128)S(1)}, f32[256,2048]{1,0:T(8,128)}, u32[]{:S(2)}) copy-start(f32[256,2048]{1,0:T(8,128)} %param.7) | copy-start | bytes 6291460
  107.3 3.3 %copy-start.1 = (f32[256,128]{1,0:T(8,128)S(1)}, f32[256,128]{1,0:T(8,128)}, u32[]{:S(2)}) copy-start(f32[256,128]{1,0:T(8,128)} %get-tuple-element.9) | copy-start | bytes 393220

commit v3 on v2

--- a/solution.py
+++ b/solution.py
@@ -268,9 +268,9 @@
         ref = own.at[pl.ds(*groups[h]), xx]
         return o2.copy(ref, ref, (d - 1, h), x_dev(d))
 
-    def t_copies():
-        far_dev = y_dev(4)
-        return (tc.copy(tout, tin, 0, far_dev), tc.copy(iout, iin, 1, far_dev))
+    def t_copy(i):
+        src, dst = (iout, iin) if i == 2 else (tout.at[i], tin.at[i])
+        return tc.copy(src, dst, i, y_dev(4))
 
     def rows_here():
         o1_home().wait()
@@ -439,10 +439,14 @@
             nh, nl = split(nt3(th, tl, ih, il))
             diag[...] = (diagonal(nxt) - past_n) - nt3(nh, nl, nh, nl)
 
-        @pl.when(j == 3)
-        def _():
-            for copy in t_copies():
-                copy.start()
+        @pl.when(j == 2)
+        def _():
+            t_copy(0).start()
+
+        @pl.when(j == 4)
+        def _():
+            t_copy(1).start()
+            t_copy(2).start()
 
         @pl.when((j >= 1) & (j < 5))
         def _():
@@ -494,8 +498,11 @@
     pass_rows(6)
     pass_more(5)
 
-    for copy in t_copies():
-        copy.wait_recv()
+    pass_more(6)
+    pass_rows(7)
+
+    for i in range(3):
+        t_copy(i).wait_recv()
     for j in range(6):
         rows_arrived(j)
 
@@ -522,8 +529,6 @@
         return 0
 
     lax.fori_loop(0, 8, first, 0)
-    pass_more(6)
-    pass_rows(7)
     for zz in range(8):
         @pl.when(jnp.logical_not(p1_self(zz)))
         def _():
@@ -547,8 +552,8 @@
         @pl.when(jnp.logical_not(m1_self(k)))
         def _():
             m1_copy(k).wait_send()
-    for copy in t_copies():
-        copy.wait_send()
+    for i in range(3):
+        t_copy(i).wait_send()
 
     def sent(j, _):
         for d in range(1, 4):
@@ -584,7 +589,7 @@
     smem = pl.BlockSpec(memory_space=pltpu.SMEM)
     vmem = pl.BlockSpec(memory_space=pltpu.VMEM)
     dma = pltpu.SemaphoreType.DMA
-    pairs = [(8,), (7, 4), (3, 5), (5,), (7,), (3, 3), (8,), (3, 3), (2,), (3, 8), (2, 8), (2, 8)]
+    pairs = [(8,), (7, 4), (3, 5), (5,), (7,), (3, 3), (8,), (3, 3), (3,), (3, 8), (2, 8), (2, 8)]
     delta, panel = pl.pallas_call(
         front_kernel,
         in_specs=[smem] * 3 + [vmem] * 3,

time: 111 us -> 107 us (0.964)
  Pallas kernels: 106 us -> 102 us
    pallas_call x1, Pallas kernels: 106 us -> 102 us  [body(): pl.pallas_call(front_kernel, in_specs=[smem] * 3 + [vmem] * 3, out_specs=...]
where the time goes in v3:
time: 107 us
  Pallas kernels  102 us (95%)
  other arithmetic  3.28 us (3%)
  between operations  1.31 us (1%)
    pallas_call x1, Pallas kernels, body(): pl.pallas_call(front_kernel, in_specs=[smem] * 3 + [vmem] * 3, out_specs=...  102 us
    add x1, other arithmetic, body(): return (front_trail + delta, panel)  3.28 us

profile of v3, /device:TPU:5, one launch (start us, length us, event | category | flops | bytes accessed | tf_op | source)
XLA Modules:
  0.0 107.1 jit_solution(11503181220415720845)
XLA Ops:
  1.3 0.0 copy-start
  1.3 101.9 %front.1 = (f32[256,2048]{1,0:T(8,128)}, f32[256,128]{1,0:T(8,128)}) custom-call(s32[1]{0:T(128)S(6)} %copy.10.mask_ref, s32[2]{0:T(128)} %bitcast.4, s32[2]{0:T(128)} %bitcast.5, f32[256,128]{1,0:T(8,128)} %below_ref.1, f32[16,128]{1,0:T(8,128)} %pivot_ref.1, f32[2,256,256]{2,1,0:T(8,128)} %bitcast.3), custom_call_target="tpu_custom_call" | custom-call | flops 6000000000 | bytes 6000000 | tf_op jit(solution)/shard_map/front/pallas_call | solution.py:593
  103.2 0.0 copy-done
  103.2 0.0 copy-start.1
  103.2 3.3 %add.3 = f32[256,2048]{1,0:T(8,128)} add(f32[256,2048]{1,0:T(8,128)S(1)} %copy-done, f32[256,2048]{1,0:T(8,128)} %get-tuple-element.4) | non-fusion elementwise | flops 524288 | bytes 6291456 | tf_op jit(solution)/shard_map/add | solution.py:639
  106.5 0.0 copy-done.1
  106.5 0.7 copy.11
Async XLA Ops:
  1.3 101.9 %copy-start = (f32[256,2048]{1,0:T(8,128)S(1)}, f32[256,2048]{1,0:T(8,128)}, u32[]{:S(2)}) copy-start(f32[256,2048]{1,0:T(8,128)} %param.7) | copy-start | bytes 6291460
  103.2 3.3 %copy-start.1 = (f32[256,128]{1,0:T(8,128)S(1)}, f32[256,128]{1,0:T(8,128)}, u32[]{:S(2)}) copy-start(f32[256,128]{1,0:T(8,128)} %get-tuple-element.9) | copy-start | bytes 393220
